TPU v7x, 256 devices: a whole 4x4x8 slice. The times are simulated.
256 devices in a mesh: sub: 2 (over z_hi), row: 8 (over x, core), col: 16 (over z_lo, y).
Axes of the slice: x: 4, y: 4, z: 8 (z_hi: 2, z_lo: 4; z = z_hi * 4 + z_lo), core: 2. Of those that a mesh axis runs over, the one named last changes fastest.
Arguments:
- panel: float32 [65536, 512], P(('sub', 'row', 'col')), as said below
- trailing: float32 [65536, 4096], P(('sub', 'row'), 'col'), may hold values from -6 to 6
- child: float32 [2, 16384, 4096], P('sub', 'row', 'col'), may hold values from -6 to 6
- child_map: int32 [2, 64], P('sub', 'row'), may hold values from 0 to 31, as said below
- pattern: int32 [256, 16], P(('sub', 'row'), 'col'), may hold values from 0 to 1
Outputs:
- factor: float32 [65536, 512], P(('sub', 'row', 'col'))
- updated: float32 [65536, 4096], P(('sub', 'row'), 'col')
Inputs may be any that keep to these rules, and one draw needn't show every extreme that they name: `child_map`: the child block rows held by one index of row map to distinct slots; slot v means half v // 16 of sub and block v % 16 of that row index's block rows. The last entry of each such run of 8 is 16 * 2 - 1. `panel`: rows 0 to 511 form a symmetric positive definite block.
All inputs are finite; a program needn't handle non-finite values.
Results may differ from a plain program's by a relative error of at most 0.00007.
Values sent between devices are 32-bit elements; how exact they have to be, the bound alone decides.
No kernel may reach another device: no remote copies, remote signals or barrier semaphores. Data moves between devices by JAX's collectives and lax.ppermute only.
A program may use at most 128 MiB of HBM per device.

v0:
```python
import jax
import jax.numpy as jnp
from jax import lax
from jax.sharding import PartitionSpec as P


def from_root(x, axis, root):
    mine = lax.axis_index(axis) == root
    return lax.psum(jnp.where(mine, x, jnp.zeros_like(x)), axis)


def local(panel, trailing, child, child_map, pattern):
    shard_rows = panel.shape[0]
    panel_width = panel.shape[1]
    block_size = trailing.shape[1]
    pieces = max(1, panel_width // shard_rows)
    pivot_pieces = []
    for number in range(pieces):
        pivot_pieces.append(from_root(panel, ("sub", "row", "col"), number))
    pivot_top = jnp.concatenate(pivot_pieces, axis=0)
    lower_factor = jnp.linalg.cholesky(pivot_top)
    identity = jnp.eye(panel_width, dtype=jnp.float32)
    inverse = jax.scipy.linalg.solve_triangular(lower_factor, identity, lower=True)
    inverse_t = inverse.T
    col_index = lax.axis_index("col")
    group_rows = jnp.dot(
        lax.all_gather(panel, "col", axis=0, tiled=True),
        inverse_t,
        precision=lax.Precision.HIGHEST,
        preferred_element_type=jnp.float32,
    )
    own_rows = lax.dynamic_slice_in_dim(group_rows, col_index * shard_rows, shard_rows, 0)
    group_count = group_rows.shape[0]
    row_blocks = group_count // block_size
    first_row = panel_width + col_index * block_size
    owner = first_row // group_count
    in_owner = first_row % group_count
    candidate = lax.dynamic_slice_in_dim(group_rows, in_owner, block_size, 0)
    window = from_root(candidate, ("sub", "row"), owner)
    window_t = window.T
    sub_count = lax.axis_size("sub")
    child_blocks = child_map.shape[1]
    all_child, all_map = (
        lax.all_gather(child, "sub", axis=0, tiled=True),
        lax.all_gather(child_map, "sub", axis=0, tiled=True),
    )
    sub_index = lax.axis_index("sub")
    own_slots = sub_index * row_blocks + jnp.arange(row_blocks, dtype=jnp.int32)
    onehot = (own_slots[:, None] == all_map.reshape(1, sub_count * child_blocks)).astype(
        jnp.float32
    )
    child_flat = all_child.reshape(sub_count * child_blocks, block_size * block_size)
    extend = jnp.dot(
        onehot, child_flat, precision=lax.Precision.HIGHEST, preferred_element_type=jnp.float32
    )
    extend = extend.reshape(row_blocks * block_size, block_size)
    assembled = trailing + extend
    update = jnp.dot(
        group_rows, window_t, precision=lax.Precision.HIGHEST, preferred_element_type=jnp.float32
    )
    present = pattern[:, 0].astype(jnp.float32)
    masked = (update.reshape(row_blocks, block_size, block_size) * present[:, None, None]).reshape(
        group_count, block_size
    )
    updated = assembled - masked
    return (own_rows, updated)


def solution(mesh):
    return jax.shard_map(
        local,
        mesh=mesh,
        in_specs=(
            P(("sub", "row", "col"), None),
            P(("sub", "row"), "col"),
            P("sub", "row", "col"),
            P("sub", "row"),
            P(("sub", "row"), "col"),
        ),
        out_specs=(P(("sub", "row", "col"), None), P(("sub", "row"), "col")),
        check_vma=False,
    )
```

profile of v0, /device:TPU:1, one launch (start us, length us, event | category | flops | bytes accessed | tf_op | source)
XLA Modules:
  0.0 691.0 jit_solution(3431088338734765414)
XLA Ops:
  11.3 9.3 %all-gather = s32[2,1,8]{2,1,0:T(1,128)S(1)} all-gather(s32[1,1,8]{2,1,0:T(1,128)S(1)} %bitcast.63), channel_id=1, replica_groups=mesh['sub'=2,'row'=8,'col'=16] {'sub'}, dimensions={0}, use_global_device_ids=true | all-gather | bytes 96 | tf_op jit(solution)/shard_map/all_gather | solution.py:45
  21.9 250.8 %all-reduce.7.cloned.1.call-done = (f32[256,512]{0,1:T(8,128)}, f32[256,512]{0,1:T(8,128)}) async-done(((f32[256,512]{0,1:T(8,128)}, f32[256,512]{0,1:T(8,128)}), (f32[256,512]{0,1:T(8,128)}, f32[256,512]{0,1:T(8,128)})) %all-reduce.7.cloned.1.call-update) | async-done | bytes 1048592 | tf_op jit(solution)/shard_map/psum | solution.py:9
  276.5 11.7 %cholesky.104 = f32[128,128]{1,0:T(8,128)S(1)} custom-call(f32[128,128]{1,0:T(8,128)S(1)} %cholesky.266), custom_call_target="Cholesky" | custom-call | tf_op jit(solution)/shard_map/jit(cholesky)/cholesky | solution.py:21
  288.4 9.8 %custom-call.31 = f32[1,128,128]{1,2,0:T(8,128)S(1)} custom-call(f32[1,128,128]{2,1,0:T(8,128)S(1)} %get-tuple-element.39), custom_call_target="InvertDiagBlocksLowerTriangular" | custom-call | tf_op jit(solution)/shard_map/jit(cholesky)/cholesky | solution.py:21
  300.7 11.7 %cholesky.217 = f32[128,128]{1,0:T(8,128)S(1)} custom-call(f32[128,128]{1,0:T(8,128)S(1)} %cholesky.270), custom_call_target="Cholesky" | custom-call | tf_op jit(solution)/shard_map/jit(cholesky)/cholesky | solution.py:21
  312.5 10.0 %custom-call.32 = f32[1,128,128]{1,2,0:T(8,128)S(1)} custom-call(f32[1,128,128]{2,1,0:T(8,128)S(1)} %get-tuple-element.36), custom_call_target="InvertDiagBlocksLowerTriangular" | custom-call | tf_op jit(solution)/shard_map/jit(cholesky)/cholesky | solution.py:21
  322.7 1.3 convolution_subtract_fusion.4
  324.0 11.7 %cholesky.238 = f32[128,128]{1,0:T(8,128)S(1)} custom-call(f32[128,128]{1,0:T(8,128)S(1)} %cholesky.275), custom_call_target="Cholesky" | custom-call | tf_op jit(solution)/shard_map/jit(cholesky)/cholesky | solution.py:21
  336.4 9.8 %custom-call.33 = f32[1,128,128]{1,2,0:T(8,128)S(1)} custom-call(f32[1,128,128]{2,1,0:T(8,128)S(1)} %get-tuple-element.33), custom_call_target="InvertDiagBlocksLowerTriangular" | custom-call | tf_op jit(solution)/shard_map/jit(cholesky)/cholesky | solution.py:21
  347.7 11.7 %cholesky.255 = f32[128,128]{1,0:T(8,128)S(1)} custom-call(f32[128,128]{1,0:T(8,128)S(1)} %convolution_subtract_fusion.5), custom_call_target="Cholesky" | custom-call | tf_op jit(solution)/shard_map/jit(cholesky)/cholesky | solution.py:21
  363.6 10.4 %while.1 = (s32[]{:T(128)}, f32[512,512]{1,0:T(8,128)S(1)}, s32[4,2]{0,1:T(2,128)S(1)}, f32[4,128,128]{2,1,0:T(8,128)}, s32[]{:T(128)}) while((s32[]{:T(128)}, f32[512,512]{1,0:T(8,128)S(1)}, s32[4,2]{0,1:T(2,128)S(1)}, f32[4,128,128]{2,1,0:T(8,128)}, s32[]{:T(128)}) %tuple.35), condition=%wide.while_cond, body=%wide.while_body.sunk | while | flops 2 | bytes 132705 | solution.py:23
  364.2 2.0 bitcast_dynamic-update-slice_fusion.2
  366.8 2.0 bitcast_dynamic-update-slice_fusion.2
  369.4 2.0 bitcast_dynamic-update-slice_fusion.2
  372.0 2.0 bitcast_dynamic-update-slice_fusion.2
  374.0 40.1 %custom-call.34 = f32[4,128,128]{1,2,0:T(8,128)S(1)} custom-call(f32[4,128,128]{2,1,0:T(8,128)} %get-tuple-element.9), custom_call_target="InvertDiagBlocksLowerTriangular" | custom-call | tf_op jit(solution)/shard_map/jit(_solve_triangular)/triangular_solve | solution.py:23
  418.9 16.7 %fusion.1 = f32[512,4096]{1,0:T(8,128)S(1)} fusion(f32[4096,512]{1,0:T(8,128)} %all-gather.4.cloned.1.call-done, f32[128,512]{1,0:T(8,128)S(1)} %fusion.29, f32[128,512]{1,0:T(8,128)S(1)} %fusion.30, f32[128,512]{1,0:T(8,128)S(1)} %fusion.32, f32[128,512]{1,0:T(8,128)S(1)} %fusion.20), kind=kOutput, calls=%fused_computation.13 | convolution fusion | flops 12885688320 | bytes 17825792 | tf_op jit(solution)/shard_map/dot_general | solution.py:26
  435.7 3.2 copy-done
  439.9 48.6 %all-gather.6.cloned.1.call-done = f32[2,2048,256]{2,1,0:T(8,128)} async-done(((f32[1,2048,256]{2,1,0:T(8,128)}), f32[2,2048,256]{2,1,0:T(8,128)}) %all-gather.6.cloned.1.call-update) | async-done | bytes 4194320 | tf_op jit(solution)/shard_map/all_gather | solution.py:44
  488.5 4.0 reshape.64
  492.5 6.3 fusion.38
  498.8 3.9 reshape.65
  503.7 160.9 %all-reduce.5.cloned.1.call-done = f32[256,512]{0,1:T(8,128)} async-done(((f32[256,512]{0,1:T(8,128)}), f32[256,512]{0,1:T(8,128)}) %all-reduce.5.cloned.1.call-update) | async-done | bytes 524304 | tf_op jit(solution)/shard_map/psum | solution.py:9
  664.6 19.4 %fusion = f32[4096,256]{1,0:T(8,128)} fusion(f32[512,4096]{1,0:T(8,128)} %copy-done, f32[256,512]{0,1:T(8,128)} %all-reduce.5.cloned.1.call-done, f32[4096,256]{1,0:T(8,128)} %param.6, f32[4096,256]{1,0:T(8,128)} %reshape.65, f32[4096]{0:T(1024)S(1)} %bitcast.62), kind=kOutput, calls=%fused_computation.3 | convolution fusion | flops 6445596672 | bytes 21512192 | tf_op jit(solution)/shard_map/dot_general | solution.py:58
  (70 shorter events, 24.8 us)
Async XLA Ops:
  7.2 4.2 copy-start.3
  7.2 14.6 %copy-start.4 = (s32[16,1]{0,1:T(1,128)S(1)}, s32[16,1]{0,1:T(1,128)}, u32[]{:S(2)}) copy-start(s32[16,1]{0,1:T(1,128)} %param.9) | copy-start | bytes 196
  7.2 265.5 %all-reduce.7.cloned.1.call-start = ((), (), s32[]{:S(2)}) async-start(), calls=%async_computation.3 | async-start | bytes 2097152 | tf_op jit(solution)/shard_map/psum | solution.py:9
  9.6 409.4 %all-gather.4.cloned.1.call-start = ((), (), s32[]{:S(2)}) async-start(), calls=%async_computation | async-start | bytes 8912896 | tf_op jit(solution)/shard_map/all_gather | solution.py:27
  10.3 478.2 %all-gather.6.cloned.1.call-start = ((), (), s32[]{:S(2)}) async-start(), calls=%async_computation.1 | async-start | bytes 6291456 | tf_op jit(solution)/shard_map/all_gather | solution.py:44
  11.0 653.6 %all-reduce.5.cloned.1.call-start = ((), (), s32[]{:S(2)}) async-start(), calls=%async_computation.2 | async-start | bytes 1048576 | tf_op jit(solution)/shard_map/psum | solution.py:9
  275.5 1.0 copy-start.1
  414.1 0.7 copy-start.2
  435.7 3.2 copy-start
Sparse Core Ops, SparseCore 0:
  14.2 258.4 all-reduce.6
  274.6 102.7 all-gather.3
  379.3 109.1 all-gather.5
  491.1 173.4 all-reduce.4
where the time goes:
time: 701 us; the launch traced here: 691 us
  waiting for transfers between devices  462 us (66%)
  other arithmetic  122 us (17%)
  matrix products  52.6 us (8%)
  local copies, waits for them, and re-layouts  28.1 us (4%)
  between operations  17.1 us (2%)
  blocking collectives  9.32 us (1%)
    psum x2, waiting for transfers between devices, from_root(): return lax.psum(jnp.where(mine, x, jnp.zeros_like(x)), axis)  412 us
    another operation x14, other arithmetic, local(): lower_factor = jnp.linalg.cholesky(pivot_top)  78.7 us
    all_gather x1, waiting for transfers between devices, local(): lax.all_gather(child, 'sub', axis=0, tiled=True)  48.6 us
    another operation x3, other arithmetic, local(): jax.scipy.linalg.solve_triangular(lower_factor, identity, lower=True)  40.3 us
    dot_general x1, matrix products, local(): jnp.dot(group_rows, window_t, precision=lax.Precision.HIGHEST, preferred_...  19.4 us
    dot_general x1, matrix products, local(): jnp.dot(lax.all_gather(panel, 'col', axis=0, tiled=True), inverse_t, prec...  16.7 us
  transfers between devices with their start and end apart: 4, of which 3 were waited for; matrix products, arithmetic and copies ran while one was open for 26% of the time, Pallas kernels for 0%

commit v1 on v0

--- a/solution.py
+++ b/solution.py
@@ -41,7 +41,9 @@
     sub_count = lax.axis_size("sub")
     child_blocks = child_map.shape[1]
     all_child, all_map = (
-        lax.all_gather(child, "sub", axis=0, tiled=True),
+        jnp.concatenate(
+            lax.all_to_all(jnp.stack([child] * lax.axis_size("sub")), "sub", 0, 0), axis=0
+        ),
         lax.all_gather(child_map, "sub", axis=0, tiled=True),
     )
     sub_index = lax.axis_index("sub")

time: 701 us -> 789 us (1.13)
  blocking collectives: 9.32 us -> 101 us
  waiting for transfers between devices: 462 us -> 445 us
  starting transfers between devices: 0.16 us -> 9.22 us
    all_gather x1, blocking collectives: 9.32 us -> 101 us  [local(): lax.all_gather(child_map, 'sub', axis=0, tiled=True)]
    all_gather x1 -> x0, waiting for transfers between devices: 48.6 us -> none  [local(): lax.all_gather(child, 'sub', axis=0, tiled=True)]
    psum x2, waiting for transfers between devices: 412 us -> 444 us  [from_root(): return lax.psum(jnp.where(mine, x, jnp.zeros_like(x)), axis)]
    all_to_all x0 -> x1, starting transfers between devices: none -> 9.14 us  [local(): lax.all_to_all(jnp.stack([child] * lax.axis_size('sub')), 'sub', 0, 0)]
  transfers between devices with their start and end apart: 4 -> 4, of which waited for: 3 -> 2; matrix products, arithmetic and copies ran while one was open for 26% -> 23% of each run, Pallas kernels for 0% -> 0%
where the time goes in v1:
time: 789 us; the launch traced here: 780 us
  waiting for transfers between devices  445 us (56%)
  other arithmetic  125 us (16%)
  blocking collectives  101 us (13%)
  matrix products  52.6 us (7%)
  local copies, waits for them, and re-layouts  28.3 us (4%)
  between operations  18.8 us (2%)
  starting transfers between devices  9.22 us (1%)
    psum x2, waiting for transfers between devices, from_root(): return lax.psum(jnp.where(mine, x, jnp.zeros_like(x)), axis)  444 us
    all_gather x1, blocking collectives, local(): lax.all_gather(child_map, 'sub', axis=0, tiled=True)  101 us
    another operation x14, other arithmetic, local(): lower_factor = jnp.linalg.cholesky(pivot_top)  78.8 us
    another operation x3, other arithmetic, local(): jax.scipy.linalg.solve_triangular(lower_factor, identity, lower=True)  40.3 us
    dot_general x1, matrix products, local(): jnp.dot(group_rows, window_t, precision=lax.Precision.HIGHEST, preferred_...  19.4 us
    dot_general x1, matrix products, local(): jnp.dot(lax.all_gather(panel, 'col', axis=0, tiled=True), inverse_t, prec...  16.7 us
  transfers between devices with their start and end apart: 4, of which 2 were waited for; matrix products, arithmetic and copies ran while one was open for 23% of the time, Pallas kernels for 0%

profile of v1, /device:TPU:1, one launch (start us, length us, event | category | flops | bytes accessed | tf_op | source)
XLA Modules:
  0.0 779.6 jit_solution(3217717697652396664)
XLA Ops:
  11.1 2.3 pad_maximum_fusion
  13.4 9.1 %all-to-all-start = ((f32[2,1,2048,256]{3,2,1,0:T(8,128)}), f32[2,1,2048,256]{3,2,1,0:T(8,128)}, u32[]{:S(2)}, u32[]{:S(2)}) async-start(f32[2,1,2048,256]{3,2,1,0:T(8,128)} %pad_maximum_fusion), calls=%async_computation | async-start | bytes 8388608 | tf_op jit(solution)/shard_map/all_to_all | solution.py:45
  22.6 101.2 %all-gather = s32[2,1,8]{2,1,0:T(1,128)S(1)} all-gather(s32[1,1,8]{2,1,0:T(1,128)S(1)} %bitcast.67), channel_id=1, replica_groups=mesh['sub'=2,'row'=8,'col'=16] {'sub'}, dimensions={0}, use_global_device_ids=true | all-gather | bytes 96 | tf_op jit(solution)/shard_map/all_gather | solution.py:47
  125.4 281.7 %all-reduce.7.cloned.1.call-done = (f32[256,512]{0,1:T(8,128)}, f32[256,512]{0,1:T(8,128)}) async-done(((f32[256,512]{0,1:T(8,128)}, f32[256,512]{0,1:T(8,128)}), (f32[256,512]{0,1:T(8,128)}, f32[256,512]{0,1:T(8,128)})) %all-reduce.7.cloned.1.call-update) | async-done | bytes 1048592 | tf_op jit(solution)/shard_map/psum | solution.py:9
  411.0 11.7 %cholesky.104 = f32[128,128]{1,0:T(8,128)S(1)} custom-call(f32[128,128]{1,0:T(8,128)S(1)} %cholesky.266), custom_call_target="Cholesky" | custom-call | tf_op jit(solution)/shard_map/jit(cholesky)/cholesky | solution.py:21
  422.9 9.8 %custom-call.31 = f32[1,128,128]{1,2,0:T(8,128)S(1)} custom-call(f32[1,128,128]{2,1,0:T(8,128)S(1)} %get-tuple-element.39), custom_call_target="InvertDiagBlocksLowerTriangular" | custom-call | tf_op jit(solution)/shard_map/jit(cholesky)/cholesky | solution.py:21
  435.2 11.7 %cholesky.217 = f32[128,128]{1,0:T(8,128)S(1)} custom-call(f32[128,128]{1,0:T(8,128)S(1)} %cholesky.270), custom_call_target="Cholesky" | custom-call | tf_op jit(solution)/shard_map/jit(cholesky)/cholesky | solution.py:21
  447.0 10.1 %custom-call.32 = f32[1,128,128]{1,2,0:T(8,128)S(1)} custom-call(f32[1,128,128]{2,1,0:T(8,128)S(1)} %get-tuple-element.36), custom_call_target="InvertDiagBlocksLowerTriangular" | custom-call | tf_op jit(solution)/shard_map/jit(cholesky)/cholesky | solution.py:21
  458.7 11.7 %cholesky.238 = f32[128,128]{1,0:T(8,128)S(1)} custom-call(f32[128,128]{1,0:T(8,128)S(1)} %cholesky.275), custom_call_target="Cholesky" | custom-call | tf_op jit(solution)/shard_map/jit(cholesky)/cholesky | solution.py:21
  470.4 9.8 %custom-call.33 = f32[1,128,128]{1,2,0:T(8,128)S(1)} custom-call(f32[1,128,128]{2,1,0:T(8,128)S(1)} %get-tuple-element.33), custom_call_target="InvertDiagBlocksLowerTriangular" | custom-call | tf_op jit(solution)/shard_map/jit(cholesky)/cholesky | solution.py:21
  481.7 11.9 %cholesky.255 = f32[128,128]{1,0:T(8,128)S(1)} custom-call(f32[128,128]{1,0:T(8,128)S(1)} %convolution_subtract_fusion.5), custom_call_target="Cholesky" | custom-call | tf_op jit(solution)/shard_map/jit(cholesky)/cholesky | solution.py:21
  498.2 10.3 %while.1 = (s32[]{:T(128)}, f32[512,512]{1,0:T(8,128)S(1)}, s32[4,2]{0,1:T(2,128)S(1)}, f32[4,128,128]{2,1,0:T(8,128)}, s32[]{:T(128)}) while((s32[]{:T(128)}, f32[512,512]{1,0:T(8,128)S(1)}, s32[4,2]{0,1:T(2,128)S(1)}, f32[4,128,128]{2,1,0:T(8,128)}, s32[]{:T(128)}) %tuple.35), condition=%wide.while_cond, body=%wide.while_body.sunk | while | flops 2 | bytes 132205 | solution.py:23
  498.9 2.0 bitcast_dynamic-update-slice_fusion.2
  501.4 2.0 bitcast_dynamic-update-slice_fusion.2
  504.0 2.0 bitcast_dynamic-update-slice_fusion.2
  506.6 2.0 bitcast_dynamic-update-slice_fusion.2
  508.6 40.1 %custom-call.34 = f32[4,128,128]{1,2,0:T(8,128)S(1)} custom-call(f32[4,128,128]{2,1,0:T(8,128)} %get-tuple-element.9), custom_call_target="InvertDiagBlocksLowerTriangular" | custom-call | tf_op jit(solution)/shard_map/jit(_solve_triangular)/triangular_solve | solution.py:23
  553.5 16.7 %fusion.1 = f32[512,4096]{1,0:T(8,128)S(1)} fusion(f32[4096,512]{1,0:T(8,128)} %all-gather.3.cloned.1.call-done, f32[128,512]{1,0:T(8,128)S(1)} %fusion.29, f32[128,512]{1,0:T(8,128)S(1)} %fusion.30, f32[128,512]{1,0:T(8,128)S(1)} %fusion.32, f32[128,512]{1,0:T(8,128)S(1)} %fusion.20), kind=kOutput, calls=%fused_computation.14 | convolution fusion | flops 12885688320 | bytes 17825792 | tf_op jit(solution)/shard_map/dot_general | solution.py:26
  570.2 3.2 copy-done
  574.4 4.0 reshape_reshape.3
  578.4 6.3 fusion.38
  584.7 3.9 reshape.61
  589.6 162.8 %all-reduce.5.cloned.1.call-done = f32[256,512]{0,1:T(8,128)} async-done(((f32[256,512]{0,1:T(8,128)}), f32[256,512]{0,1:T(8,128)}) %all-reduce.5.cloned.1.call-update) | async-done | bytes 524304 | tf_op jit(solution)/shard_map/psum | solution.py:9
  752.4 19.4 %fusion = f32[4096,256]{1,0:T(8,128)} fusion(f32[512,4096]{1,0:T(8,128)} %copy-done, f32[256,512]{0,1:T(8,128)} %all-reduce.5.cloned.1.call-done, f32[4096,256]{1,0:T(8,128)} %param.6, f32[4096,256]{1,0:T(8,128)} %reshape.61, f32[4096]{0:T(1024)S(1)} %bitcast.66), kind=kOutput, calls=%fused_computation.3 | convolution fusion | flops 6445596672 | bytes 21512192 | tf_op jit(solution)/shard_map/dot_general | solution.py:60
  (72 shorter events, 25.5 us)
Async XLA Ops:
  8.0 3.1 copy-start.2
  8.0 399.1 %all-reduce.7.cloned.1.call-start = ((), (), s32[]{:S(2)}) async-start(), calls=%async_computation.3 | async-start | bytes 2097152 | tf_op jit(solution)/shard_map/psum | solution.py:9
  10.5 543.0 %all-gather.3.cloned.1.call-start = ((), (), s32[]{:S(2)}) async-start(), calls=%async_computation.1 | async-start | bytes 8912896 | tf_op jit(solution)/shard_map/all_gather | solution.py:27
  13.4 9.1 %copy-start.4 = (s32[1,8]{1,0:T(1,128)S(1)}, s32[1,8]{1,0:T(1,128)}, u32[]{:S(2)}) copy-start(s32[1,8]{1,0:T(1,128)} %param.8) | copy-start | bytes 100
  13.4 111.7 %copy-start.5 = (s32[16,1]{0,1:T(1,128)S(1)}, s32[16,1]{0,1:T(1,128)}, u32[]{:S(2)}) copy-start(s32[16,1]{0,1:T(1,128)} %param.9) | copy-start | bytes 196
  13.4 561.0 %all-to-all-start = ((f32[2,1,2048,256]{3,2,1,0:T(8,128)}), f32[2,1,2048,256]{3,2,1,0:T(8,128)}, u32[]{:S(2)}, u32[]{:S(2)}) async-start(f32[2,1,2048,256]{3,2,1,0:T(8,128)} %pad_maximum_fusion), calls=%async_computation | async-start | bytes 8388608 | tf_op jit(solution)/shard_map/all_to_all | solution.py:45
  22.6 729.8 %all-reduce.5.cloned.1.call-start = ((), (), s32[]{:S(2)}) async-start(), calls=%async_computation.2 | async-start | bytes 1048576 | tf_op jit(solution)/shard_map/psum | solution.py:9
  409.9 1.1 copy-start.1
  548.7 0.7 copy-start.3
  570.2 3.2 copy-start
Sparse Core Ops, SparseCore 0:
  15.0 392.0 all-reduce.6
  574.5 177.8 all-reduce.4
Sparse Core Ops, SparseCore 1:
  12.8 193.8 all-gather.2
